TPU v7x, 256 devices: a whole 4x4x8 slice. The times are simulated.
256 devices in a mesh: row: 16 (over y, z_lo, core), col: 16 (over z_hi, x).
Axes of the slice: x: 4, y: 4, z: 8 (z_hi: 4, z_lo: 2; z = z_hi * 2 + z_lo), core: 2. Of those that a mesh axis runs over, the one named last changes fastest.
Arguments:
- gradient: bfloat16 [1024, 25600], P('row', 'col'), may hold values from -6 to 6
- basis: bfloat16 [25600, 25600], P('col', 'row'), may hold values from -0.0390625 to 0.0390625
- moment: float32 [1024, 25600], P('col', 'row'), may hold values from -2 to 2
- second: float32 [1024, 25600], P('col', 'row'), may hold values from 0.05 to 2
Outputs:
- new_moment: float32 [1024, 25600], P('col', 'row')
- new_second: float32 [1024, 25600], P('col', 'row')
- direction: bfloat16 [1024, 25600], P('row', 'col')
All inputs are finite; a program needn't handle non-finite values.
Results may differ from a plain program's by a relative error of at most 0.0048.
Values may be sent and summed in bfloat16 or wider, within the bound.
A program may use at most 64 MiB of HBM per device.

v0:
```python
import jax
import jax.numpy as jnp
from jax import lax
from jax.sharding import PartitionSpec as P

beta_one = 0.9
beta_two = 0.95
bias_one = 1.0 - 0.9**10
bias_two = 1.0 - 0.95**10
epsilon = 1e-08


def adam_update(rotated, moment, second):
    new_moment = beta_one * moment + (1.0 - beta_one) * rotated
    new_second = beta_two * second + (1.0 - beta_two) * rotated * rotated
    scaled = (new_moment / bias_one / (jnp.sqrt(new_second / bias_two) + epsilon)).astype(
        jnp.bfloat16
    )
    return (new_moment, new_second, scaled)


def rotate_forward(gathered, basis_part):
    return lax.psum_scatter(
        jnp.dot(gathered, basis_part, preferred_element_type=jnp.float32),
        "col",
        scatter_dimension=0,
        tiled=True,
    )


def on_device(gradient, basis, moment, second):
    gathered = lax.all_gather(gradient, "row", axis=0, tiled=True)
    basis_part = basis
    rotated = rotate_forward(gathered, basis_part)
    new_moment, new_second, scaled = adam_update(rotated, moment, second)
    moment_parts = new_moment
    second_parts = new_second
    spread = lax.all_gather(scaled, "col", axis=0, tiled=True)
    spread, basis_part = (spread, basis_part)
    product = lax.dot_general(
        spread, basis_part, (((1,), (1,)), ((), ())), preferred_element_type=jnp.float32
    )
    direction = lax.psum_scatter(product, "row", scatter_dimension=0, tiled=True).astype(
        jnp.bfloat16
    )
    new_moment = moment_parts
    new_second = second_parts
    return (new_moment, new_second, direction)


def solution(mesh):
    return jax.shard_map(
        on_device,
        mesh=mesh,
        in_specs=(P("row", "col"), P("col", "row"), P("col", "row"), P("col", "row")),
        out_specs=(P("col", "row"), P("col", "row"), P("row", "col")),
        check_vma=False,
    )
```

profile of v0, /device:TPU:1, one launch (start us, length us, event | category | flops | bytes accessed | tf_op | source)
XLA Modules:
  0.0 351.6 jit_solution(8847891839872214190)
XLA Ops:
  7.2 0.0 all-gather.3.cloned.1.call-start
  7.2 0.7 all-gather.3.cloned.1.call-update
  7.9 0.0 reduce-scatter.3.cloned.1.call-start
  7.9 45.1 %all-gather.3.cloned.1.call-done = bf16[1024,1600]{1,0:T(8,128)(2,1)} async-done(((bf16[64,1600]{1,0:T(8,128)(2,1)}), bf16[1024,1600]{1,0:T(8,128)(2,1)}) %all-gather.3.cloned.1.call-update) | async-done | bytes 3276816 | tf_op jit(solution)/shard_map/all_gather | solution.py:32
  53.1 11.7 %fusion.2 = f32[1024,1600]{1,0:T(8,128)} fusion(bf16[1024,1600]{1,0:T(8,128)(2,1)} %all-gather.3.cloned.1.call-done, bf16[1600,1600]{1,0:T(8,128)(2,1)} %param.5), kind=kOutput, calls=%fused_computation.4 | convolution fusion | flops 5242880000 | bytes 14950400 | tf_op jit(solution)/shard_map/dot_general | solution.py:24
  64.8 0.0 copy-start
  64.8 0.0 copy-start.1
  64.8 0.0 reduce-scatter.3.cloned.1.call-update
  64.8 0.0 all-gather.5.cloned.1.call-start
  64.9 112.2 %reduce-scatter.3.cloned.1.call-done = f32[64,1600]{1,0:T(8,128)} async-done(((f32[1024,1600]{1,0:T(8,128)}), f32[64,1600]{1,0:T(8,128)}) %reduce-scatter.3.cloned.1.call-update) | async-done | bytes 409616 | tf_op jit(solution)/shard_map/reduce_scatter | solution.py:23
  177.0 0.0 copy-done
  177.0 0.0 copy-done.1
  177.0 2.1 divide_convert_fusion
  179.1 0.0 all-gather.5.cloned.1.call-update
  179.2 0.0 reduce-scatter.5.cloned.1.call-start
  179.2 71.3 %all-gather.5.cloned.1.call-done = bf16[1024,1600]{1,0:T(8,128)(2,1)} async-done(((bf16[64,1600]{1,0:T(8,128)(2,1)}), bf16[1024,1600]{1,0:T(8,128)(2,1)}) %all-gather.5.cloned.1.call-update) | async-done | bytes 3276816 | tf_op jit(solution)/shard_map/all_gather | solution.py:38
  250.5 11.8 %fusion.3 = f32[1024,1600]{1,0:T(8,128)} fusion(bf16[1024,1600]{1,0:T(8,128)(2,1)} %all-gather.5.cloned.1.call-done, bf16[1600,1600]{1,0:T(8,128)(2,1)} %param.5), kind=kOutput, calls=%fused_computation.5 | convolution fusion | flops 5242880000 | bytes 14950400 | tf_op jit(solution)/shard_map/dot_general | solution.py:40
  262.3 0.0 reduce-scatter.5.cloned.1.call-update
  262.3 81.1 %reduce-scatter.5.cloned.1.call-done = f32[64,1600]{1,0:T(8,128)} async-done(((f32[1024,1600]{1,0:T(8,128)}), f32[64,1600]{1,0:T(8,128)}) %reduce-scatter.5.cloned.1.call-update) | async-done | bytes 409616 | tf_op jit(solution)/shard_map/reduce_scatter | solution.py:43
  343.4 1.7 convert_element_type.7
Async XLA Ops:
  7.2 45.9 %all-gather.3.cloned.1.call-start = ((), (), s32[]{:S(2)}) async-start(), calls=%async_computation.2 | async-start | bytes 3620864 | tf_op jit(solution)/shard_map/all_gather | solution.py:32
  7.9 169.1 %reduce-scatter.3.cloned.1.call-start = ((), (), s32[]{:S(2)}) async-start(), calls=%async_computation.3 | async-start | bytes 7241728 | tf_op jit(solution)/shard_map/reduce_scatter | solution.py:23
  64.8 112.2 %copy-start = (f32[64,1600]{1,0:T(8,128)S(1)}, f32[64,1600]{1,0:T(8,128)}, u32[]{:S(2)}) copy-start(f32[64,1600]{1,0:T(8,128)} %param.7) | copy-start | bytes 1228804
  64.8 112.2 %copy-start.1 = (f32[64,1600]{1,0:T(8,128)S(1)}, f32[64,1600]{1,0:T(8,128)}, u32[]{:S(2)}) copy-start(f32[64,1600]{1,0:T(8,128)} %param.6) | copy-start | bytes 1228804
  64.8 185.7 %all-gather.5.cloned.1.call-start = ((), (), s32[]{:S(2)}) async-start(), calls=%async_computation.4 | async-start | bytes 3620864 | tf_op jit(solution)/shard_map/all_gather | solution.py:38
  179.2 164.2 %reduce-scatter.5.cloned.1.call-start = ((), (), s32[]{:S(2)}) async-start(), calls=%async_computation.5 | async-start | bytes 7241728 | tf_op jit(solution)/shard_map/reduce_scatter | solution.py:43
Sparse Core Ops, SparseCore 0:
  9.8 43.1 all-gather.2
  64.9 112.0 reduce-scatter.2
  180.3 70.1 all-gather.4
  262.4 80.8 reduce-scatter.4
where the time goes:
time: 353 us; the launch traced here: 352 us
  waiting for transfers between devices  310 us (88%)
  matrix products  23.5 us (7%)
  between operations  13.8 us (4%)
  other arithmetic  3.83 us (1%)
    reduce_scatter x1, waiting for transfers between devices, rotate_forward(): lax.psum_scatter(jnp.dot(gathered, basis_part, preferred_element_type=jnp...  112 us
    reduce_scatter x1, waiting for transfers between devices, on_device(): lax.psum_scatter(product, 'row', scatter_dimension=0, tiled=True)  81.1 us
    all_gather x1, waiting for transfers between devices, on_device(): spread = lax.all_gather(scaled, 'col', axis=0, tiled=True)  71.3 us
    all_gather x1, waiting for transfers between devices, on_device(): gathered = lax.all_gather(gradient, 'row', axis=0, tiled=True)  45.1 us
    dot_general x1, matrix products, on_device(): lax.dot_general(spread, basis_part, (((1,), (1,)), ((), ())), preferred_e...  11.8 us
    dot_general x1, matrix products, rotate_forward(): jnp.dot(gathered, basis_part, preferred_element_type=jnp.float32)  11.7 us
  transfers between devices with their start and end apart: 4, of which 4 were waited for; matrix products, arithmetic and copies ran while one was open for 0% of the time, Pallas kernels for 0%

commit v1 on v0

v1 whole, which is shorter than its diff:
```python
import functools

import jax
import jax.numpy as jnp
from jax import lax
from jax.experimental import pallas as pl
from jax.experimental.pallas import tpu as pltpu
from jax.sharding import PartitionSpec as P

MESH = pl.DeviceIdType.MESH
F32, BF16 = jnp.float32, jnp.bfloat16

beta_one = 0.9
beta_two = 0.95
bias_one = 1.0 - 0.9**10
bias_two = 1.0 - 0.95**10
epsilon = 1e-08

N = 1600
Q = 4
T = 16
TILES = [(j, min(256, N - j)) for j in range(0, N, 256)]

KINDS = ("g", "cf", "A", "B", "C", "D", "E1", "E2", "F", "G", "H", "I")
ROWS = dict(g=112, cf=128, A=64, B=128, C=48, D=48, E1=64, E2=64, F=64, G=128, H=96, I=16)

ORDER = [(0, 'g'), (1, 'g'), (0, 'cf'), (2, 'g'), (0, 'm1'), (3, 'g'), (1, 'cf'), (0, 'a'), (1, 'm1'), (2, 'cf'),
         (3, 'cf'), (0, 'b'), (1, 'a'), (2, 'm1'), (1, 'b'), (2, 'a'), (0, 'ad'), (3, 'm1'), (1, 'ad'), (3, 'a'),
         (0, 'e'), (2, 'b'), (3, 'b'), (1, 'e'), (0, 'f'), (2, 'ad'), (1, 'f'), (0, 'm2'), (3, 'ad'), (1, 'm2'),
         (2, 'e'), (0, 'h'), (2, 'f'), (1, 'h'), (3, 'e'), (2, 'm2'), (3, 'f'), (0, 'i'), (2, 'h'), (1, 'i'),
         (3, 'm2'), (3, 'h'), (2, 'i'), (3, 'i'), (1, 'o'), (0, 'o'), (2, 'o'), (3, 'o')]


def kernel(
    grad, basis, moment, second, new_moment, new_second, direction,
    bv, mv, sv, nmv, nsv, dv,
    gath, part, part16, a_in, b_out, b_in, c_out, c_own, c_in, step, g_in, h_out, h_own, h_in, i_own, i_out, i_in,
    send, recv, local,
):
    row, col = lax.axis_index("row"), lax.axis_index("col")
    core, zlo, y = row % 2, (row // 2) % 2, row // 4
    x, zhi = col % 4, col // 4

    def at_row(yy, zz, cc):
        return ((yy * 2 + zz) * 2 + cc, col)

    def at_col(zz, xx):
        return (row, zz * 4 + xx)

    x_up, x_down, x_far = (x + 1) % 4, (x + 3) % 4, (x + 2) % 4
    right, left = at_col(zhi, x_up), at_col(zhi, x_down)
    sibling = at_row(y, zlo, 1 - core)
    partner = at_row(y, 1 - zlo, core)
    peers_z = [at_col((zhi + d) % 4, x) for d in (1, 2, 3)]
    peers_y = [at_row((y + d) % 4, zlo, core) for d in (1, 2, 3)]
    peers_row = [partner] + [at_row((y + d) % 4, z, core) for d in (1, 2, 3) for z in (0, 1)]

    def ds(start, size):
        return pl.ds(pl.multiple_of(start, 16), size)

    mine = ((zlo * 2 + core) * 4 + y) * T
    own = [
        pltpu.make_async_copy(grad.at[pl.ds(q * T, T)], gath.at[q, ds(mine, T)], local.at[q]) for q in range(Q)
    ]
    for c in own:
        c.start()
    load_b = pltpu.make_async_copy(basis, bv, local.at[4])
    load_m = pltpu.make_async_copy(moment, mv, local.at[5])
    load_s = pltpu.make_async_copy(second, sv, local.at[6])
    load_b.start()
    load_m.start()
    load_s.start()

    barrier = pltpu.get_barrier_semaphore()
    partners = [right, left, sibling] + peers_z + peers_row
    for d in partners:
        pl.semaphore_signal(barrier, inc=1, device_id=d, device_id_type=MESH)
    pl.semaphore_wait(barrier, len(partners))

    def put(kind, q, src, dst, to):
        k = KINDS.index(kind)
        pltpu.make_async_remote_copy(
            src_ref=src, dst_ref=dst, send_sem=send.at[k, q], recv_sem=recv.at[k, q], device_id=to, device_id_type=MESH
        ).start()

    def span(kind):
        ref = g_in if kind == "G" else part16
        return ref.at[0, pl.ds(0, ROWS[kind])]

    def got(kind, q):
        pltpu.make_async_copy(span(kind), span(kind), recv.at[KINDS.index(kind), q]).wait()

    def sent(kind, q):
        pltpu.make_async_copy(span(kind), span(kind), send.at[KINDS.index(kind), q]).wait()

    def gather(q):
        own[q].wait()
        for d in peers_row:
            block = gath.at[q, ds(mine, T)]
            put("g", q, block, block, d)

    def gather_core(q):
        got("g", q)
        for z in (0, 1):
            block = gath.at[q, ds((z * 2 + core) * 64, 64)]
            put("cf", q, block, block, sibling)

    def forward(q):
        got("cf", q)
        if q == 0:
            load_b.wait()
        for j, w in TILES:
            p = jnp.dot(gath[q], bv[:, j : j + w], preferred_element_type=F32)
            part[q, :, j : j + w] = p
            part16[q, :, j : j + w] = p.astype(BF16)
        put("A", q, part16.at[q, ds(x_far * 64, 32)], a_in.at[q, pl.ds(0, 32)], right)
        put("A", q, part16.at[q, ds(x_far * 64 + 32, 32)], a_in.at[q, pl.ds(32, 32)], left)
        put("B", q, part16.at[q, ds(x_up * 64 + 32, 32)], b_in.at[q, pl.ds(32, 32)], right)
        put("B", q, part16.at[q, ds(x_down * 64, 32)], b_in.at[q, pl.ds(64, 32)], left)

    def add_far(q):
        got("A", q)
        for half, start in ((0, x_up * 64), (1, x_down * 64 + 32)):
            for i in range(0, 32, T):
                at = half * 32 + i
                b_out[q, at : at + T] = (
                    part[q, ds(start + i, T)] + a_in[q, at : at + T].astype(F32)
                ).astype(BF16)
        put("B", q, b_out.at[q, pl.ds(0, 32)], b_in.at[q, pl.ds(0, 32)], right)
        put("B", q, b_out.at[q, pl.ds(32, 32)], b_in.at[q, pl.ds(96, 32)], left)

    def sum_x(q, i):
        return (
            part[q, ds(x * 64 + i, T)]
            + b_in[q, ds(i, T)].astype(F32)
            + b_in[q, ds(64 + i, T)].astype(F32)
        )

    def add_x(q):
        got("B", q)
        for i in range(0, 64, T):
            c_out[q, i : i + T] = sum_x(q, i).astype(BF16)
        for d in (1, 2, 3):
            put("C", q, c_out.at[q, ds((zhi + d) % 4 * T, T)], c_in.at[q, pl.ds((d - 1) * T, T)], peers_z[d - 1])
        c_own[q] = sum_x(q, zhi * T)

    def adam(q):
        if q == 0:
            load_m.wait()
            load_s.wait()
        got("C", q)
        rotated = c_own[q]
        for d in range(3):
            rotated += c_in[q, d * T : d * T + T].astype(F32)
        rows = slice(q * T, q * T + T)
        nm = beta_one * mv[rows] + (1.0 - beta_one) * rotated
        ns = beta_two * sv[rows] + (1.0 - beta_two) * rotated * rotated
        nmv[rows] = nm
        nsv[rows] = ns
        block = step.at[q, ds(x * 64 + zhi * T, T)]
        block[...] = (nm / bias_one / (jnp.sqrt(ns / bias_two) + epsilon)).astype(BF16)
        for d in peers_z:
            put("D", q, block, block, d)

    def spread(q):
        got("D", q)
        first, last = (step.at[q, ds(x * 64 + i, 32)] for i in (0, 32))
        put("E1", q, first, first, right)
        put("E1", q, last, last, left)
        put("E2", q, last, last, right)
        put("E2", q, first, first, left)

    def spread_far(q):
        got("E1", q)
        first, last = step.at[q, ds(x_down * 64, 32)], step.at[q, ds(x_up * 64 + 32, 32)]
        put("F", q, first, first, right)
        put("F", q, last, last, left)

    def back(q):
        got("E2", q)
        got("F", q)
        for j, w in TILES:
            part[q, :, j : j + w] = lax.dot_general(
                step[q], bv[j : j + w, :], (((1,), (1,)), ((), ())), preferred_element_type=F32
            )
        for z in (0, 1):
            put("G", q, part.at[q, ds((z * 2 + 1 - core) * 64, 64)], g_in.at[q, pl.ds(z * 64, 64)], sibling)

    def add_core(q):
        got("G", q)

        def total(z, yy):
            return part[q, ds((z * 2 + core) * 64 + yy * T, T)] + g_in[q, ds(z * 64 + yy * T, T)]

        for yy in range(4):
            for z in (0, 1):
                at = (yy * 2 + z) * T
                h_out[q, at : at + T] = total(z, yy).astype(BF16)
        for d in (1, 2, 3):
            put("H", q, h_out.at[q, ds((y + d) % 4 * 32, 32)], h_in.at[q, pl.ds((d - 1) * 32, 32)], peers_y[d - 1])
        for z in (0, 1):
            h_own[q, z * T : z * T + T] = total(z, y)

    def add_y(q):
        got("H", q)

        def total(z):
            t = h_own[q, ds(z * T, T)]
            for d in range(3):
                t += h_in[q, ds(d * 32 + z * T, T)].astype(F32)
            return t

        i_out[q] = total(1 - zlo).astype(BF16)
        put("I", q, i_out.at[q], i_in.at[q], partner)
        i_own[q] = total(zlo)

    def finish(q):
        got("I", q)
        dv[q * T : q * T + T] = (i_own[q] + i_in[q].astype(F32)).astype(BF16)

    phases = dict(
        g=gather, cf=gather_core, m1=forward, a=add_far, b=add_x, ad=adam, e=spread, f=spread_far, m2=back, h=add_core,
        i=add_y, o=finish,
    )
    moments = [
        pltpu.make_async_copy(nmv, new_moment, local.at[7]),
        pltpu.make_async_copy(nsv, new_second, local.at[8]),
    ]
    left_over = set(range(Q))
    for q, name in ORDER:
        phases[name](q)
        if name == "ad":
            left_over.remove(q)
            if not left_over:
                for c in moments:
                    c.start()
    out = pltpu.make_async_copy(dv, direction, local.at[9])
    out.start()
    for q in range(Q):
        for kind in KINDS:
            sent(kind, q)
    for c in moments:
        c.wait()
    out.wait()


def on_device(gradient, basis, moment, second):
    def vm(rows, dtype=BF16):
        return pltpu.VMEM((Q, rows, N), dtype)

    small = [pltpu.VMEM((Q * T, N), F32)] * 4 + [pltpu.VMEM((Q * T, N), BF16)]
    anywhere = pl.BlockSpec(memory_space=pl.ANY)
    return pl.pallas_call(
        kernel,
        out_shape=[
            jax.ShapeDtypeStruct((Q * T, N), F32),
            jax.ShapeDtypeStruct((Q * T, N), F32),
            jax.ShapeDtypeStruct((Q * T, N), BF16),
        ],
        in_specs=[anywhere] * 4,
        out_specs=[anywhere] * 3,
        scratch_shapes=[pltpu.VMEM((N, N), BF16)] + small + [
            vm(256), vm(256, F32), vm(256), vm(64), vm(64), vm(128), vm(64), vm(T, F32), vm(48), vm(256),
            vm(128, F32), vm(128), vm(32, F32), vm(96), vm(T, F32), vm(T), vm(T),
            pltpu.SemaphoreType.DMA((len(KINDS), Q)),
            pltpu.SemaphoreType.DMA((len(KINDS), Q)),
            pltpu.SemaphoreType.DMA((10,)),
        ],
        compiler_params=pltpu.CompilerParams(
            collective_id=0, has_side_effects=True, vmem_limit_bytes=58 * 1024 * 1024
        ),
        cost_estimate=pl.CostEstimate(flops=4 * 1024 * N * N, bytes_accessed=8 << 20, transcendentals=0),
        name="soap_step",
    )(gradient, basis, moment, second)


def solution(mesh):
    return jax.shard_map(
        on_device,
        mesh=mesh,
        in_specs=(P("row", "col"), P("col", "row"), P("col", "row"), P("col", "row")),
        out_specs=(P("col", "row"), P("col", "row"), P("row", "col")),
        check_vma=False,
    )
```

time: 353 us -> 111 us (0.31)
  waiting for transfers between devices: 310 us -> 0 us
  Pallas kernels: 0 us -> 105 us
  matrix products: 23.5 us -> 0 us
  between operations: 13.8 us -> 0.64 us
  local copies, waits for them, and re-layouts: 0.01 us -> 5.21 us
  other arithmetic: 3.83 us -> 0 us
    reduce_scatter x2 -> x0, waiting for transfers between devices: 193 us -> none  [the longest x1 112 us: rotate_forward(): lax.psum_scatter(jnp.dot(gathered, basis_part, preferred_element_type=jnp...]
    all_gather x2 -> x0, waiting for transfers between devices: 116 us -> none  [the longest x1 71.3 us: on_device(): spread = lax.all_gather(scaled, 'col', axis=0, tiled=True)]
    pallas_call x0 -> x1, Pallas kernels: none -> 105 us  [on_device(): pl.pallas_call(kernel, out_shape=[jax.ShapeDtypeStruct((Q * T, N), F32),...]
    dot_general x2 -> x0, matrix products: 23.5 us -> none  [the longest x1 11.8 us: on_device(): lax.dot_general(spread, basis_part, (((1,), (1,)), ((), ())), preferred_e...]
    unnamed x4 -> x3, local copies, waits for them, and re-layouts: 0.01 us -> 5.21 us
    convert_element_type x2 -> x0, other arithmetic: 3.83 us -> none  [the longest x1 2.12 us: adam_update(): (new_moment / bias_one / (jnp.sqrt(new_second / bias_two) + epsilon)).ast...]
  transfers between devices with their start and end apart: 4 -> 0, of which waited for: 4 -> 0; matrix products, arithmetic and copies ran while one was open for 0% -> 0% of each run, Pallas kernels for 0% -> 0%
where the time goes in v1:
time: 111 us
  Pallas kernels  105 us (95%)
  local copies, waits for them, and re-layouts  5.21 us (5%)
    pallas_call x1, Pallas kernels, on_device(): pl.pallas_call(kernel, out_shape=[jax.ShapeDtypeStruct((Q * T, N), F32),...  105 us
    unnamed x3, local copies, waits for them, and re-layouts  5.21 us

profile of v1, /device:TPU:1, one launch (start us, length us, event | category | flops | bytes accessed | tf_op | source)
XLA Modules:
  0.0 110.7 jit_solution(17465345097728871856)
XLA Ops:
  0.6 104.9 %soap_step.1 = (f32[64,1600]{1,0:T(8,128)}, f32[64,1600]{1,0:T(8,128)}, bf16[64,1600]{1,0:T(8,128)(2,1)}) custom-call(bf16[64,1600]{1,0:T(8,128)(2,1)} %grad.1, bf16[1600,1600]{1,0:T(8,128)(2,1)} %basis.1, f32[64,1600]{1,0:T(8,128)} %moment.1, f32[64,1600]{1,0:T(8,128)} %second.1), custom_call_target="tpu_custom_call" | custom-call | flops 10485760000 | bytes 8388608 | tf_op jit(solution)/shard_map/soap_step/pallas_call | solution.py:253
  105.5 1.8 %copy.10 = f32[64,1600]{1,0:T(8,128)} copy(f32[64,1600]{1,0:T(8,128)} %get-tuple-element.6) | data formatting | bytes 819200
  107.3 1.8 %copy.11 = f32[64,1600]{1,0:T(8,128)} copy(f32[64,1600]{1,0:T(8,128)} %get-tuple-element.7) | data formatting | bytes 819200
  109.1 1.6 %copy.12 = bf16[64,1600]{1,0:T(8,128)(2,1)} copy(bf16[64,1600]{1,0:T(8,128)(2,1)} %get-tuple-element.8) | data formatting | bytes 409600

commit v2 on v0

v2 whole, which is shorter than its diff:
```python
import jax
import jax.numpy as jnp
from jax import lax
from jax.experimental import pallas as pl
from jax.experimental.pallas import tpu as pltpu
from jax.sharding import PartitionSpec as P

MESH = pl.DeviceIdType.MESH
F32, BF16 = jnp.float32, jnp.bfloat16

beta_one = 0.9
beta_two = 0.95
bias_one = 1.0 - 0.9**10
bias_two = 1.0 - 0.95**10
epsilon = 1e-08

N = 1600
Q = 4
T = 16
SPLIT = [(0, 768), (768, 832)]
J = len(SPLIT)


def tiles(start, size):
    return [(j, min(256, start + size - j)) for j in range(start, start + size, 256)]


ROWS = dict(g=112, cf=128, A=64, B=128, C=48, D=48, E1=64, E2=64, F=64, G=128, H=112)
KINDS = tuple(ROWS)
WHOLE = ("g", "cf", "G", "H")


ORDER = [
    (0, "g", 0), (1, "g", 0), (2, "g", 0), (0, "cf", 0), (3, "g", 0), (0, "m1", 0), (0, "m1", 1), (1, "cf", 0),
    (0, "a", 0), (1, "m1", 0), (0, "a", 1), (0, "b", 0), (2, "cf", 0), (1, "a", 0), (1, "m1", 1), (0, "b", 1),
    (3, "cf", 0), (2, "m1", 0), (1, "b", 0), (1, "a", 1), (3, "m1", 0), (0, "ad", 0), (3, "m1", 1), (0, "ad", 1),
    (1, "ad", 0), (3, "a", 0), (2, "a", 0), (1, "b", 1), (2, "m1", 1), (3, "b", 0), (3, "a", 1), (0, "e", 0),
    (2, "b", 0), (2, "a", 1), (3, "b", 1), (1, "e", 0), (1, "ad", 1), (0, "e", 1), (1, "f", 0), (3, "ad", 0),
    (2, "b", 1), (0, "f", 0), (0, "f", 1), (2, "ad", 0), (1, "e", 1), (3, "e", 0), (0, "m2", 0), (3, "ad", 1),
    (1, "m2", 0), (1, "f", 1), (0, "m2", 1), (3, "f", 0), (2, "ad", 1), (2, "e", 0), (0, "h", 1), (3, "e", 1),
    (1, "m2", 1), (3, "m2a", 0), (2, "f", 0), (2, "e", 1), (1, "h", 1), (3, "f", 1), (3, "m2b", 0), (3, "m2a", 1),
    (2, "m2", 0), (2, "f", 1), (3, "ha", 1), (3, "m2b", 1), (2, "m2", 1), (3, "hb", 1), (1, "o", 1), (0, "o", 1),
    (2, "h", 1), (3, "o", 1), (2, "o", 1),
]


def kernel(
    grad, basis, moment, second, nmv, nsv, dv,
    bv, mv, sv, gath, part, part16, a_in, b_out, b_in, c_out, c_own, c_in, step, g_in, h_out, h_own, h_in,
    send, recv, recv_g, local,
):
    row, col = lax.axis_index("row"), lax.axis_index("col")
    core, zlo, y = row % 2, (row // 2) % 2, row // 4
    x, zhi = col % 4, col // 4

    def at_row(yy, zz, cc):
        return ((yy * 2 + zz) * 2 + cc, col)

    def at_col(zz, xx):
        return (row, zz * 4 + xx)

    x_up, x_down, x_far = (x + 1) % 4, (x + 3) % 4, (x + 2) % 4
    right, left = at_col(zhi, x_up), at_col(zhi, x_down)
    sibling = at_row(y, zlo, 1 - core)
    partner = at_row(y, 1 - zlo, core)
    peers_z = [at_col((zhi + d) % 4, x) for d in (1, 2, 3)]
    peers_row = [partner] + [at_row((y + d) % 4, z, core) for d in (1, 2, 3) for z in (0, 1)]

    def ds(start, size):
        return pl.ds(pl.multiple_of(start, 16), size)

    def cols(j):
        return pl.ds(*SPLIT[j])

    mine = ((zlo * 2 + core) * 4 + y) * T
    own = [
        pltpu.make_async_copy(grad.at[pl.ds(q * T, T)], gath.at[q, ds(mine, T)], local.at[q]) for q in range(Q)
    ]
    for c in own:
        c.start()
    load_b = pltpu.make_async_copy(basis, bv, local.at[4])
    load_m = pltpu.make_async_copy(moment, mv, local.at[5])
    load_s = pltpu.make_async_copy(second, sv, local.at[6])
    load_b.start()
    load_m.start()
    load_s.start()

    barrier = pltpu.get_barrier_semaphore()
    partners = [right, left, sibling] + peers_z + peers_row
    for d in partners:
        pl.semaphore_signal(barrier, inc=1, device_id=d, device_id_type=MESH)
    pl.semaphore_wait(barrier, len(partners))

    def put(kind, sem, src, dst, to):
        pltpu.make_async_remote_copy(
            src_ref=src, dst_ref=dst, send_sem=send.at[KINDS.index(kind)], recv_sem=sem, device_id=to,
            device_id_type=MESH,
        ).start()

    def arrival(kind, q, j=0):
        return recv.at[KINDS.index(kind), q, j]

    def await_rows(sem, ref):
        pltpu.make_async_copy(ref, ref, sem).wait()

    def got(kind, q, j=0):
        span = part16.at[0, pl.ds(0, ROWS[kind])]
        if kind not in WHOLE:
            span = part16.at[0, pl.ds(0, ROWS[kind]), cols(j)]
        await_rows(arrival(kind, q, j), span)

    def sent(kind):
        ref = part if kind == "G" else part16
        await_rows(send.at[KINDS.index(kind)], ref.at[:, pl.ds(0, ROWS[kind])])

    def gather(q, j):
        own[q].wait()
        for d in peers_row:
            block = gath.at[q, ds(mine, T)]
            put("g", arrival("g", q), block, block, d)

    def gather_core(q, j):
        got("g", q)
        for z in (0, 1):
            block = gath.at[q, ds((z * 2 + core) * 64, 64)]
            put("cf", arrival("cf", q), block, block, sibling)

    def forward(q, j):
        if j == 0:
            got("cf", q)
            if q == 0:
                load_b.wait()
        for s, w in tiles(*SPLIT[j]):
            p = jnp.dot(gath[q], bv[:, s : s + w], preferred_element_type=F32)
            part[q, :, s : s + w] = p
            part16[q, :, s : s + w] = p.astype(BF16)
        c = cols(j)
        for kind, block, ref, at, to in (
            ("A", x_far * 64, a_in, 0, right),
            ("A", x_far * 64 + 32, a_in, 32, left),
            ("B", x_up * 64 + 32, b_in, 32, right),
            ("B", x_down * 64, b_in, 64, left),
        ):
            put(kind, arrival(kind, q, j), part16.at[q, ds(block, 32), c], ref.at[q, pl.ds(at, 32), c], to)

    def add_far(q, j):
        got("A", q, j)
        c = cols(j)
        for half, start in ((0, x_up * 64), (1, x_down * 64 + 32)):
            for i in range(0, 32, T):
                at = half * 32 + i
                b_out[q, at : at + T, c] = (
                    part[q, ds(start + i, T), c] + a_in[q, at : at + T, c].astype(F32)
                ).astype(BF16)
        put("B", arrival("B", q, j), b_out.at[q, pl.ds(0, 32), c], b_in.at[q, pl.ds(0, 32), c], right)
        put("B", arrival("B", q, j), b_out.at[q, pl.ds(32, 32), c], b_in.at[q, pl.ds(96, 32), c], left)

    def add_x(q, j):
        got("B", q, j)
        c = cols(j)

        def total(i):
            return (
                part[q, ds(x * 64 + i, T), c] + b_in[q, ds(i, T), c].astype(F32) + b_in[q, ds(64 + i, T), c].astype(F32)
            )

        for i in range(0, 64, T):
            c_out[q, i : i + T, c] = total(i).astype(BF16)
        for d in (1, 2, 3):
            put(
                "C", arrival("C", q, j), c_out.at[q, ds((zhi + d) % 4 * T, T), c],
                c_in.at[q, pl.ds((d - 1) * T, T), c], peers_z[d - 1],
            )
        c_own[q, :, c] = total(zhi * T)

    def adam(q, j):
        if q == 0 and j == 0:
            load_m.wait()
            load_s.wait()
        got("C", q, j)
        c = cols(j)
        rotated = c_own[q, :, c]
        for d in range(3):
            rotated += c_in[q, d * T : d * T + T, c].astype(F32)
        rows = pl.ds(q * T, T)
        nm = beta_one * mv[rows, c] + (1.0 - beta_one) * rotated
        ns = beta_two * sv[rows, c] + (1.0 - beta_two) * rotated * rotated
        nmv[rows, c] = nm
        nsv[rows, c] = ns
        block = step.at[q, ds(64 + zhi * T, T), c]
        block[...] = (nm / bias_one / (jnp.sqrt(ns / bias_two) + epsilon)).astype(BF16)
        for d in peers_z:
            put("D", arrival("D", q, j), block, block, d)

    def rows_of(q, j, start):
        return step.at[q, pl.ds(start, 32), cols(j)]

    def spread(q, j):
        got("D", q, j)
        put("E1", arrival("E1", q, j), rows_of(q, j, 64), rows_of(q, j, 0), right)
        put("E1", arrival("E1", q, j), rows_of(q, j, 96), rows_of(q, j, 160), left)
        put("E2", arrival("E2", q, j), rows_of(q, j, 96), rows_of(q, j, 32), right)
        put("E2", arrival("E2", q, j), rows_of(q, j, 64), rows_of(q, j, 128), left)

    def spread_far(q, j):
        got("E1", q, j)
        put("F", arrival("F", q, j), rows_of(q, j, 0), rows_of(q, j, 192), right)
        put("F", arrival("F", q, j), rows_of(q, j, 160), rows_of(q, j, 224), left)

    def back(q, j, first, size):
        rows = pl.ds(first, size)
        for s, w in tiles(0, N):
            d = lax.dot_general(
                step[q, rows, cols(j)], bv[s : s + w, cols(j)], (((1,), (1,)), ((), ())), preferred_element_type=F32
            )
            if j:
                d += part[q, rows, s : s + w]
            part[q, rows, s : s + w] = d

    def slot(dest):
        return (dest - x + 5) % 4 * 64

    def give_core(q, z):
        put(
            "G", recv_g.at[q, z], part.at[q, ds(slot(z * 2 + 1 - core), 64)], g_in.at[q, pl.ds(z * 64, 64)], sibling
        )

    def add_core(q, z):
        await_rows(recv_g.at[q, z], g_in.at[q, pl.ds(0, 64)])

        def total(yy):
            return part[q, ds(slot(z * 2 + core) + yy * T, T)] + g_in[q, ds(z * 64 + yy * T, T)]

        other = (z + zlo) % 2
        for d in range(4):
            yy = (y + d) % 4

            def pass_on(d=d, yy=yy):
                at = z * 64 + d * T
                h_out[q, ds(at, T)] = total(yy).astype(BF16)
                put(
                    "H", arrival("H", q), h_out.at[q, ds(at, T)], h_in.at[q, ds(other * 64 + d * T, T)],
                    at_row(yy, z, core),
                )

            if d:
                pass_on()
            else:
                pl.when(other == 1)(pass_on)

                @pl.when(other == 0)
                def _():
                    h_own[q] = total(y)

    def back_all(q, j):
        if j == 0:
            got("E2", q, 0)
            got("F", q, 0)
        else:
            got("E2", q, 1)
            got("F", q, 1)
        back(q, j, 0, 256)
        if j == J - 1:
            for z in (0, 1):
                give_core(q, z)

    def add_all(q, j):
        for z in (0, 1):
            add_core(q, z)

    def back_near(q, j):
        got("E2", q, j)
        back(q, j, 0, 192)
        if j == J - 1:
            for z in (0, 1):
                pl.when(z * 2 + 1 - core != x_far)(lambda z=z: give_core(q, z))

    def add_near(q, j):
        for z in (0, 1):
            pl.when(z * 2 + core != x_far)(lambda z=z: add_core(q, z))

    def back_far(q, j):
        got("F", q, j)
        back(q, j, 192, 64)
        if j == J - 1:
            for z in (0, 1):
                pl.when(z * 2 + 1 - core == x_far)(lambda z=z: give_core(q, z))

    def add_rest(q, j):
        for z in (0, 1):
            pl.when(z * 2 + core == x_far)(lambda z=z: add_core(q, z))

    def finish(q, j):
        got("H", q)
        total = h_own[q]
        for i in range(1, 8):
            total += h_in[q, i * T : i * T + T].astype(F32)
        dv[q * T : q * T + T] = total.astype(BF16)

    phases = dict(
        g=gather, cf=gather_core, m1=forward, a=add_far, b=add_x, ad=adam, e=spread, f=spread_far,
        m2=back_all, h=add_all, m2a=back_near, ha=add_near, m2b=back_far, hb=add_rest, o=finish,
    )
    for q, name, j in ORDER:
        phases[name](q, j)
    for kind in KINDS:
        sent(kind)


def flush(a, b, c, out_a, out_b, out_c, sems):
    copies = [
        pltpu.make_async_copy(src, dst, sems.at[i])
        for i, (src, dst) in enumerate(((a, out_a), (b, out_b), (c, out_c)))
    ]
    for copy in copies:
        copy.start()
    for copy in copies:
        copy.wait()


def on_device(gradient, basis, moment, second):
    def vm(rows, dtype=BF16):
        return pltpu.VMEM((Q, rows, N), dtype)

    anywhere = pl.BlockSpec(memory_space=pl.ANY)
    in_vmem = pl.BlockSpec(memory_space=pltpu.VMEM)
    shapes = [((Q * T, N), F32), ((Q * T, N), F32), ((Q * T, N), BF16)]
    results = pl.pallas_call(
        kernel,
        out_shape=[pltpu.VMEM(*s) for s in shapes],
        in_specs=[anywhere] * 4,
        out_specs=[in_vmem] * 3,
        scratch_shapes=[pltpu.VMEM((N, N), BF16)] + [pltpu.VMEM((Q * T, N), F32)] * 2 + [
            vm(256), vm(256, F32), vm(256), vm(64), vm(64), vm(128), vm(64), vm(T, F32), vm(48), vm(256),
            vm(128, F32), vm(128), vm(T, F32), vm(128),
            pltpu.SemaphoreType.DMA((len(KINDS),)),
            pltpu.SemaphoreType.DMA((len(KINDS), Q, J)),
            pltpu.SemaphoreType.DMA((Q, 2)),
            pltpu.SemaphoreType.DMA((7,)),
        ],
        compiler_params=pltpu.CompilerParams(
            collective_id=0, has_side_effects=True, vmem_limit_bytes=56 * 1024 * 1024
        ),
        cost_estimate=pl.CostEstimate(flops=4 * 1024 * N * N, bytes_accessed=8 << 20, transcendentals=0),
        name="soap_step",
    )(gradient, basis, moment, second)
    return pl.pallas_call(
        flush,
        out_shape=[jax.ShapeDtypeStruct(*s) for s in shapes],
        in_specs=[in_vmem] * 3,
        out_specs=[anywhere] * 3,
        scratch_shapes=[pltpu.SemaphoreType.DMA((3,))],
        name="flush",
    )(*results)


def solution(mesh):
    return jax.shard_map(
        on_device,
        mesh=mesh,
        in_specs=(P("row", "col"), P("col", "row"), P("col", "row"), P("col", "row")),
        out_specs=(P("col", "row"), P("col", "row"), P("row", "col")),
        check_vma=False,
    )
```

time: 353 us -> 97.6 us (0.28)
  waiting for transfers between devices: 310 us -> 0 us
  Pallas kernels: 0 us -> 94.5 us
  matrix products: 23.5 us -> 0 us
  between operations: 13.8 us -> 0.81 us
  other arithmetic: 3.83 us -> 0 us
    reduce_scatter x2 -> x0, waiting for transfers between devices: 193 us -> none  [the longest x1 112 us: rotate_forward(): lax.psum_scatter(jnp.dot(gathered, basis_part, preferred_element_type=jnp...]
    all_gather x2 -> x0, waiting for transfers between devices: 116 us -> none  [the longest x1 71.3 us: on_device(): spread = lax.all_gather(scaled, 'col', axis=0, tiled=True)]
    pallas_call x0 -> x2, Pallas kernels: none -> 94.5 us  [the longest x1 92.3 us: on_device(): pl.pallas_call(kernel, out_shape=[pltpu.VMEM(*s) for s in shapes], in_spe...]
    dot_general x2 -> x0, matrix products: 23.5 us -> none  [the longest x1 11.8 us: on_device(): lax.dot_general(spread, basis_part, (((1,), (1,)), ((), ())), preferred_e...]
    convert_element_type x2 -> x0, other arithmetic: 3.83 us -> none  [the longest x1 2.12 us: adam_update(): (new_moment / bias_one / (jnp.sqrt(new_second / bias_two) + epsilon)).ast...]
  transfers between devices with their start and end apart: 4 -> 0, of which waited for: 4 -> 0; matrix products, arithmetic and copies ran while one was open for 0% -> 0% of each run, Pallas kernels for 0% -> 0%
where the time goes in v2:
time: 97.6 us; the launch traced here: 97.5 us
  Pallas kernels  94.5 us (97%)
  local copies, waits for them, and re-layouts  2.2 us (2%)
    pallas_call x1, Pallas kernels, on_device(): pl.pallas_call(kernel, out_shape=[pltpu.VMEM(*s) for s in shapes], in_spe...  92.3 us
    unnamed x6, local copies, waits for them, and re-layouts  2.2 us
    pallas_call x1, Pallas kernels, on_device(): pl.pallas_call(flush, out_shape=[jax.ShapeDtypeStruct(*s) for s in shapes...  2.18 us

profile of v2, /device:TPU:1, one launch (start us, length us, event | category | flops | bytes accessed | tf_op | source)
XLA Modules:
  0.0 97.5 jit_solution(4206847689952803629)
XLA Ops:
  0.6 92.3 %soap_step.1 = (f32[64,1600]{1,0:T(8,128)S(1)}, f32[64,1600]{1,0:T(8,128)S(1)}, bf16[64,1600]{1,0:T(8,128)(2,1)S(1)}) custom-call(bf16[64,1600]{1,0:T(8,128)(2,1)} %grad.1, bf16[1600,1600]{1,0:T(8,128)(2,1)} %basis.1, f32[64,1600]{1,0:T(8,128)} %moment.1, f32[64,1600]{1,0:T(8,128)} %second.1), custom_call_target="tpu_custom_call" | custom-call | flops 10485760000 | bytes 8388608 | tf_op jit(solution)/shard_map/soap_step/pallas_call | solution.py:328
  92.9 0.0 copy-start
  92.9 0.7 copy-done
  93.7 0.0 copy-start.1
  93.7 0.8 copy-done.1
  94.5 0.0 copy-start.2
  94.5 0.7 copy-done.2
  95.1 2.2 %flush.1 = (f32[64,1600]{1,0:T(8,128)}, f32[64,1600]{1,0:T(8,128)}, bf16[64,1600]{1,0:T(8,128)(2,1)}) custom-call(f32[64,1600]{1,0:T(8,128)} %copy-done, f32[64,1600]{1,0:T(8,128)} %copy-done.1, bf16[64,1600]{1,0:T(8,128)(2,1)} %copy-done.2), custom_call_target="tpu_custom_call" | custom-call | tf_op jit(solution)/shard_map/flush/pallas_call | solution.py:347
Async XLA Ops:
  92.9 0.8 copy-start
  93.7 0.8 copy-start.1
  94.5 0.7 copy-start.2

commit v3 on v2

--- a/solution.py
+++ b/solution.py
@@ -25,28 +25,31 @@
     return [(j, min(256, start + size - j)) for j in range(start, start + size, 256)]
 
 
-ROWS = dict(g=112, cf=128, A=64, B=128, C=48, D=48, E1=64, E2=64, F=64, G=128, H=112)
+ROWS = dict(g=112, cf=128, A=64, B=128, C=48, D=48, E1=64, E2=64, F=64, G=128, H=112, Y=96, I=16)
 KINDS = tuple(ROWS)
-WHOLE = ("g", "cf", "G", "H")
+WHOLE = ("g", "cf", "G", "H", "Y", "I")
+
+EARLY = (0, 1)
 
 
 ORDER = [
-    (0, "g", 0), (1, "g", 0), (2, "g", 0), (0, "cf", 0), (3, "g", 0), (0, "m1", 0), (0, "m1", 1), (1, "cf", 0),
-    (0, "a", 0), (1, "m1", 0), (0, "a", 1), (0, "b", 0), (2, "cf", 0), (1, "a", 0), (1, "m1", 1), (0, "b", 1),
-    (3, "cf", 0), (2, "m1", 0), (1, "b", 0), (1, "a", 1), (3, "m1", 0), (0, "ad", 0), (3, "m1", 1), (0, "ad", 1),
-    (1, "ad", 0), (3, "a", 0), (2, "a", 0), (1, "b", 1), (2, "m1", 1), (3, "b", 0), (3, "a", 1), (0, "e", 0),
-    (2, "b", 0), (2, "a", 1), (3, "b", 1), (1, "e", 0), (1, "ad", 1), (0, "e", 1), (1, "f", 0), (3, "ad", 0),
-    (2, "b", 1), (0, "f", 0), (0, "f", 1), (2, "ad", 0), (1, "e", 1), (3, "e", 0), (0, "m2", 0), (3, "ad", 1),
-    (1, "m2", 0), (1, "f", 1), (0, "m2", 1), (3, "f", 0), (2, "ad", 1), (2, "e", 0), (0, "h", 1), (3, "e", 1),
-    (1, "m2", 1), (3, "m2a", 0), (2, "f", 0), (2, "e", 1), (1, "h", 1), (3, "f", 1), (3, "m2b", 0), (3, "m2a", 1),
-    (2, "m2", 0), (2, "f", 1), (3, "ha", 1), (3, "m2b", 1), (2, "m2", 1), (3, "hb", 1), (1, "o", 1), (0, "o", 1),
-    (2, "h", 1), (3, "o", 1), (2, "o", 1),
+    (0, "g", 0), (1, "g", 0), (0, "tr", 0), (0, "cf", 0), (2, "g", 0), (0, "m1", 0), (0, "m1", 1), (1, "cf", 0),
+    (3, "g", 0), (0, "a", 0), (1, "m1", 1), (0, "a", 1), (2, "cf", 0), (0, "b", 0), (1, "a", 1), (1, "m1", 0),
+    (2, "m1", 0), (0, "b", 1), (3, "cf", 0), (1, "b", 1), (2, "m1", 1), (1, "a", 0), (3, "m1", 0), (0, "ad", 0),
+    (0, "ad", 1), (2, "a", 1), (2, "a", 0), (3, "m1", 1), (1, "b", 0), (0, "e", 0), (1, "ad", 1), (0, "e", 1),
+    (2, "b", 1), (3, "a", 1), (1, "ad", 0), (2, "b", 0), (3, "a", 0), (0, "f", 0), (0, "f", 1), (2, "ad", 1),
+    (1, "e", 1), (3, "b", 1), (2, "ad", 0), (1, "e", 0), (0, "m2", 0), (3, "b", 0), (1, "f", 1), (0, "m2", 1),
+    (0, "gx", 0), (1, "f", 0), (2, "e", 1), (3, "ad", 1), (0, "h", 0), (1, "m2", 1), (2, "e", 0), (1, "m2", 0),
+    (1, "gx", 0), (3, "ad", 0), (2, "f", 1), (2, "m2a", 1), (2, "f", 0), (1, "h", 0), (3, "e", 1), (2, "m2a", 0),
+    (2, "ga", 0), (0, "i", 0), (2, "m2b", 1), (3, "e", 0), (2, "ha", 0), (3, "f", 1), (2, "m2b", 0), (2, "gb", 0),
+    (3, "m2a", 1), (3, "f", 0), (0, "o", 0), (2, "hb", 0), (3, "m2a", 0), (3, "ga", 0), (1, "i", 0), (3, "m2b", 1),
+    (3, "ha", 0), (3, "m2b", 0), (3, "gb", 0), (1, "o", 0), (3, "hb", 0), (2, "o", 0), (3, "o", 0),
 ]
 
 
 def kernel(
     grad, basis, moment, second, nmv, nsv, dv,
-    bv, mv, sv, gath, part, part16, a_in, b_out, b_in, c_out, c_own, c_in, step, g_in, h_out, h_own, h_in,
+    bv, bt, mv, sv, gath, part, part16, a_in, b_out, b_in, c_out, c_own, c_in, step, g_in, h_out, h_own, h_in, i_own, i_out, i_in,
     send, recv, recv_g, local,
 ):
     row, col = lax.axis_index("row"), lax.axis_index("col")
@@ -64,6 +67,7 @@
     sibling = at_row(y, zlo, 1 - core)
     partner = at_row(y, 1 - zlo, core)
     peers_z = [at_col((zhi + d) % 4, x) for d in (1, 2, 3)]
+    peers_y = [at_row((y + d) % 4, zlo, core) for d in (1, 2, 3)]
     peers_row = [partner] + [at_row((y + d) % 4, z, core) for d in (1, 2, 3) for z in (0, 1)]
 
     def ds(start, size):
@@ -72,7 +76,10 @@
     def cols(j):
         return pl.ds(*SPLIT[j])
 
-    mine = ((zlo * 2 + core) * 4 + y) * T
+    def blk(dest):
+        return (dest % 2 * 2 + dest // 2) * 64
+
+    mine = (core * 2 + zlo) * 64 + y * T
     own = [
         pltpu.make_async_copy(grad.at[pl.ds(q * T, T)], gath.at[q, ds(mine, T)], local.at[q]) for q in range(Q)
     ]
@@ -104,14 +111,17 @@
         pltpu.make_async_copy(ref, ref, sem).wait()
 
     def got(kind, q, j=0):
-        span = part16.at[0, pl.ds(0, ROWS[kind])]
+        rows = ROWS[kind]
+        span = part16.at[0, pl.ds(0, rows)]
         if kind not in WHOLE:
-            span = part16.at[0, pl.ds(0, ROWS[kind]), cols(j)]
+            span = part16.at[0, pl.ds(0, rows), cols(j)]
         await_rows(arrival(kind, q, j), span)
 
     def sent(kind):
         ref = part if kind == "G" else part16
-        await_rows(send.at[KINDS.index(kind)], ref.at[:, pl.ds(0, ROWS[kind])])
+        chunks = {"H": Q - len(EARLY), "Y": len(EARLY), "I": len(EARLY)}.get(kind, Q)
+        span = ref.at[pl.ds(0, chunks), pl.ds(0, ROWS[kind])]
+        await_rows(send.at[KINDS.index(kind)], span)
 
     def gather(q, j):
         own[q].wait()
@@ -121,32 +131,65 @@
 
     def gather_core(q, j):
         got("g", q)
-        for z in (0, 1):
-            block = gath.at[q, ds((z * 2 + core) * 64, 64)]
-            put("cf", arrival("cf", q), block, block, sibling)
+        block = gath.at[q, ds(core * 128, 128)]
+        put("cf", arrival("cf", q), block, block, sibling)
+
+    def transpose(q, j):
+        load_b.wait()
+        for s, w in tiles(0, N):
+            for c, v in tiles(0, N):
+                bt[c : c + v, s : s + w] = bv[s : s + w, c : c + v].T
+
+    seen = set()
+
+    def first(*key):
+        new = key not in seen
+        seen.add(key)
+        return new
+
+    def multiply(q, j, rows):
+        for s, w in tiles(*SPLIT[j]):
+            p = jnp.dot(gath[q, rows], bv[:, s : s + w], preferred_element_type=F32)
+            part[q, rows, s : s + w] = p
+            part16[q, rows, s : s + w] = p.astype(BF16)
+
+    def send_half(kind, q, j, block, ref, at, to):
+        c = cols(j)
+        put(kind, arrival(kind, q, j), part16.at[q, ds(block, 32), c], ref.at[q, pl.ds(at, 32), c], to)
+
+    def send_far(q, j):
+        send_half("A", q, j, blk(x_far), a_in, 0, right)
+        send_half("A", q, j, blk(x_far) + 32, a_in, 32, left)
+
+    def send_near(q, j):
+        send_half("B", q, j, blk(x_up) + 32, b_in, 32, right)
+        send_half("B", q, j, blk(x_down), b_in, 64, left)
+
+    far_first = core == x % 2
+
+    def forward_own(q, j):
+        multiply(q, j, ds(core * 128, 128))
+        pl.when(far_first)(lambda: send_far(q, j))
+        pl.when(jnp.logical_not(far_first))(lambda: send_near(q, j))
+
+    def forward_other(q, j):
+        if first("m1", q):
+            got("cf", q)
+        multiply(q, j, ds((1 - core) * 128, 128))
+        pl.when(far_first)(lambda: send_near(q, j))
+        pl.when(jnp.logical_not(far_first))(lambda: send_far(q, j))
 
     def forward(q, j):
-        if j == 0:
+        if first("m1", q):
             got("cf", q)
-            if q == 0:
-                load_b.wait()
-        for s, w in tiles(*SPLIT[j]):
-            p = jnp.dot(gath[q], bv[:, s : s + w], preferred_element_type=F32)
-            part[q, :, s : s + w] = p
-            part16[q, :, s : s + w] = p.astype(BF16)
-        c = cols(j)
-        for kind, block, ref, at, to in (
-            ("A", x_far * 64, a_in, 0, right),
-            ("A", x_far * 64 + 32, a_in, 32, left),
-            ("B", x_up * 64 + 32, b_in, 32, right),
-            ("B", x_down * 64, b_in, 64, left),
-        ):
-            put(kind, arrival(kind, q, j), part16.at[q, ds(block, 32), c], ref.at[q, pl.ds(at, 32), c], to)
+        multiply(q, j, pl.ds(0, 256))
+        send_far(q, j)
+        send_near(q, j)
 
     def add_far(q, j):
         got("A", q, j)
         c = cols(j)
-        for half, start in ((0, x_up * 64), (1, x_down * 64 + 32)):
+        for half, start in ((0, blk(x_up)), (1, blk(x_down) + 32)):
             for i in range(0, 32, T):
                 at = half * 32 + i
                 b_out[q, at : at + T, c] = (
@@ -161,7 +204,7 @@
 
         def total(i):
             return (
-                part[q, ds(x * 64 + i, T), c] + b_in[q, ds(i, T), c].astype(F32) + b_in[q, ds(64 + i, T), c].astype(F32)
+                part[q, ds(blk(x) + i, T), c] + b_in[q, ds(i, T), c].astype(F32) + b_in[q, ds(64 + i, T), c].astype(F32)
             )
 
         for i in range(0, 64, T):
@@ -174,7 +217,7 @@
         c_own[q, :, c] = total(zhi * T)
 
     def adam(q, j):
-        if q == 0 and j == 0:
+        if first("moments"):
             load_m.wait()
             load_s.wait()
         got("C", q, j)
@@ -207,13 +250,12 @@
         put("F", arrival("F", q, j), rows_of(q, j, 0), rows_of(q, j, 192), right)
         put("F", arrival("F", q, j), rows_of(q, j, 160), rows_of(q, j, 224), left)
 
-    def back(q, j, first, size):
-        rows = pl.ds(first, size)
+    def back(q, j, start, size):
+        rows = pl.ds(start, size)
+        new = first("m2", q, start)
         for s, w in tiles(0, N):
-            d = lax.dot_general(
-                step[q, rows, cols(j)], bv[s : s + w, cols(j)], (((1,), (1,)), ((), ())), preferred_element_type=F32
-            )
-            if j:
+            d = jnp.dot(step[q, rows, cols(j)], bt[cols(j), s : s + w], preferred_element_type=F32)
+            if not new:
                 d += part[q, rows, s : s + w]
             part[q, rows, s : s + w] = d
 
@@ -250,30 +292,55 @@
 
                 @pl.when(other == 0)
                 def _():
-                    h_own[q] = total(y)
+                    i_own[q] = total(y)
 
     def back_all(q, j):
-        if j == 0:
-            got("E2", q, 0)
-            got("F", q, 0)
-        else:
-            got("E2", q, 1)
-            got("F", q, 1)
+        got("E2", q, j)
+        got("F", q, j)
         back(q, j, 0, 256)
-        if j == J - 1:
+
+    def give_all(q, j):
+        for z in (0, 1):
+            give_core(q, z)
+
+    def add_all(q, j):
+        for z in (0, 1):
+            await_rows(recv_g.at[q, z], g_in.at[q, pl.ds(0, 64)])
+
+        def total(z, yy):
+            return part[q, ds(slot(z * 2 + core) + yy * T, T)] + g_in[q, ds(z * 64 + yy * T, T)]
+
+        for d in (1, 2, 3):
+            yy = (y + d) % 4
             for z in (0, 1):
-                give_core(q, z)
-
-    def add_all(q, j):
-        for z in (0, 1):
-            add_core(q, z)
+                at = d * 32 + z * T
+                h_out[q, at : at + T] = total(z, yy).astype(BF16)
+            put(
+                "Y", arrival("Y", q), h_out.at[q, pl.ds(d * 32, 32)], h_in.at[q, pl.ds(d * 32, 32)], peers_y[d - 1]
+            )
+        for z in (0, 1):
+            h_own[q, z * T : z * T + T] = total(z, y)
+
+    def add_y(q, j):
+        got("Y", q)
+
+        def total(z):
+            t = h_own[q, ds(z * T, T)]
+            for d in (1, 2, 3):
+                t += h_in[q, ds(d * 32 + z * T, T)].astype(F32)
+            return t
+
+        i_out[q] = total(1 - zlo).astype(BF16)
+        put("I", arrival("I", q), i_out.at[q], i_in.at[q], partner)
+        i_own[q] = total(zlo)
 
     def back_near(q, j):
         got("E2", q, j)
         back(q, j, 0, 192)
-        if j == J - 1:
-            for z in (0, 1):
-                pl.when(z * 2 + 1 - core != x_far)(lambda z=z: give_core(q, z))
+
+    def give_near(q, j):
+        for z in (0, 1):
+            pl.when(z * 2 + 1 - core != x_far)(lambda z=z: give_core(q, z))
 
     def add_near(q, j):
         for z in (0, 1):
@@ -282,24 +349,30 @@
     def back_far(q, j):
         got("F", q, j)
         back(q, j, 192, 64)
-        if j == J - 1:
-            for z in (0, 1):
-                pl.when(z * 2 + 1 - core == x_far)(lambda z=z: give_core(q, z))
+
+    def give_far(q, j):
+        for z in (0, 1):
+            pl.when(z * 2 + 1 - core == x_far)(lambda z=z: give_core(q, z))
 
     def add_rest(q, j):
         for z in (0, 1):
             pl.when(z * 2 + core == x_far)(lambda z=z: add_core(q, z))
 
     def finish(q, j):
-        got("H", q)
-        total = h_own[q]
-        for i in range(1, 8):
-            total += h_in[q, i * T : i * T + T].astype(F32)
+        total = i_own[q]
+        if q in EARLY:
+            got("I", q)
+            total += i_in[q].astype(F32)
+        else:
+            got("H", q)
+            for i in range(1, 8):
+                total += h_in[q, i * T : i * T + T].astype(F32)
         dv[q * T : q * T + T] = total.astype(BF16)
 
     phases = dict(
-        g=gather, cf=gather_core, m1=forward, a=add_far, b=add_x, ad=adam, e=spread, f=spread_far,
-        m2=back_all, h=add_all, m2a=back_near, ha=add_near, m2b=back_far, hb=add_rest, o=finish,
+        g=gather, cf=gather_core, tr=transpose, n=forward_own, mo=forward_other, m1=forward, a=add_far, b=add_x, ad=adam, e=spread, f=spread_far,
+        m2=back_all, gx=give_all, h=add_all, i=add_y,
+        m2a=back_near, ga=give_near, ha=add_near, m2b=back_far, gb=give_far, hb=add_rest, o=finish,
     )
     for q, name, j in ORDER:
         phases[name](q, j)
@@ -330,9 +403,9 @@
         out_shape=[pltpu.VMEM(*s) for s in shapes],
         in_specs=[anywhere] * 4,
         out_specs=[in_vmem] * 3,
-        scratch_shapes=[pltpu.VMEM((N, N), BF16)] + [pltpu.VMEM((Q * T, N), F32)] * 2 + [
+        scratch_shapes=[pltpu.VMEM((N, N), BF16)] * 2 + [pltpu.VMEM((Q * T, N), F32)] * 2 + [
             vm(256), vm(256, F32), vm(256), vm(64), vm(64), vm(128), vm(64), vm(T, F32), vm(48), vm(256),
-            vm(128, F32), vm(128), vm(T, F32), vm(128),
+            vm(128, F32), vm(128), vm(32, F32), vm(128), vm(T, F32), vm(T), vm(T),
             pltpu.SemaphoreType.DMA((len(KINDS),)),
             pltpu.SemaphoreType.DMA((len(KINDS), Q, J)),
             pltpu.SemaphoreType.DMA((Q, 2)),
@@ -347,9 +420,10 @@
     return pl.pallas_call(
         flush,
         out_shape=[jax.ShapeDtypeStruct(*s) for s in shapes],
-        in_specs=[in_vmem] * 3,
+        in_specs=[anywhere] * 3,
         out_specs=[anywhere] * 3,
         scratch_shapes=[pltpu.SemaphoreType.DMA((3,))],
+        compiler_params=pltpu.CompilerParams(vmem_limit_bytes=1024 * 1024),
         name="flush",
     )(*results)
 

time: 97.6 us -> 90.8 us (0.930); the launches traced: 97.5 us -> 89.5 us
  Pallas kernels: 94.5 us -> 88.7 us
  local copies, waits for them, and re-layouts: 2.2 us -> 0 us
    pallas_call x1, Pallas kernels: 92.3 us -> 87.7 us  [on_device(): pl.pallas_call(kernel, out_shape=[pltpu.VMEM(*s) for s in shapes], in_spe...]
    unnamed x6 -> x0, local copies, waits for them, and re-layouts: 2.2 us -> none
    pallas_call x1, Pallas kernels: 2.18 us -> 0.99 us  [on_device(): pl.pallas_call(flush, out_shape=[jax.ShapeDtypeStruct(*s) for s in shapes...]
where the time goes in v3:
time: 90.8 us; the launch traced here: 89.5 us
  Pallas kernels  88.7 us (98%)
    pallas_call x1, Pallas kernels, on_device(): pl.pallas_call(kernel, out_shape=[pltpu.VMEM(*s) for s in shapes], in_spe...  87.7 us

profile of v3, /device:TPU:1, one launch (start us, length us, event | category | flops | bytes accessed | tf_op | source)
XLA Modules:
  0.0 89.5 jit_solution(12154846203708708583)
XLA Ops:
  0.6 87.7 %soap_step.1 = (f32[64,1600]{1,0:T(8,128)S(1)}, f32[64,1600]{1,0:T(8,128)S(1)}, bf16[64,1600]{1,0:T(8,128)(2,1)S(1)}) custom-call(bf16[64,1600]{1,0:T(8,128)(2,1)} %grad.1, bf16[1600,1600]{1,0:T(8,128)(2,1)} %basis.1, f32[64,1600]{1,0:T(8,128)} %moment.1, f32[64,1600]{1,0:T(8,128)} %second.1), custom_call_target="tpu_custom_call" | custom-call | flops 10485760000 | bytes 8388608 | tf_op jit(solution)/shard_map/soap_step/pallas_call | solution.py:401
  88.4 1.0 %flush.1 = (f32[64,1600]{1,0:T(8,128)}, f32[64,1600]{1,0:T(8,128)}, bf16[64,1600]{1,0:T(8,128)(2,1)}) custom-call(f32[64,1600]{1,0:T(8,128)S(1)} %get-tuple-element.6.a, f32[64,1600]{1,0:T(8,128)S(1)} %get-tuple-element.7.b, bf16[64,1600]{1,0:T(8,128)(2,1)S(1)} %get-tuple-element.8.c), custom_call_target="tpu_custom_call" | custom-call | tf_op jit(solution)/shard_map/flush/pallas_call | solution.py:420

commit v4 on v3

--- a/solution.py
+++ b/solution.py
@@ -34,16 +34,16 @@
 
 ORDER = [
     (0, "g", 0), (1, "g", 0), (0, "tr", 0), (0, "cf", 0), (2, "g", 0), (0, "m1", 0), (0, "m1", 1), (1, "cf", 0),
-    (3, "g", 0), (0, "a", 0), (1, "m1", 1), (0, "a", 1), (2, "cf", 0), (0, "b", 0), (1, "a", 1), (1, "m1", 0),
-    (2, "m1", 0), (0, "b", 1), (3, "cf", 0), (1, "b", 1), (2, "m1", 1), (1, "a", 0), (3, "m1", 0), (0, "ad", 0),
-    (0, "ad", 1), (2, "a", 1), (2, "a", 0), (3, "m1", 1), (1, "b", 0), (0, "e", 0), (1, "ad", 1), (0, "e", 1),
-    (2, "b", 1), (3, "a", 1), (1, "ad", 0), (2, "b", 0), (3, "a", 0), (0, "f", 0), (0, "f", 1), (2, "ad", 1),
-    (1, "e", 1), (3, "b", 1), (2, "ad", 0), (1, "e", 0), (0, "m2", 0), (3, "b", 0), (1, "f", 1), (0, "m2", 1),
-    (0, "gx", 0), (1, "f", 0), (2, "e", 1), (3, "ad", 1), (0, "h", 0), (1, "m2", 1), (2, "e", 0), (1, "m2", 0),
-    (1, "gx", 0), (3, "ad", 0), (2, "f", 1), (2, "m2a", 1), (2, "f", 0), (1, "h", 0), (3, "e", 1), (2, "m2a", 0),
-    (2, "ga", 0), (0, "i", 0), (2, "m2b", 1), (3, "e", 0), (2, "ha", 0), (3, "f", 1), (2, "m2b", 0), (2, "gb", 0),
-    (3, "m2a", 1), (3, "f", 0), (0, "o", 0), (2, "hb", 0), (3, "m2a", 0), (3, "ga", 0), (1, "i", 0), (3, "m2b", 1),
-    (3, "ha", 0), (3, "m2b", 0), (3, "gb", 0), (1, "o", 0), (3, "hb", 0), (2, "o", 0), (3, "o", 0),
+    (3, "g", 0), (0, "a", 0), (1, "m1", 1), (2, "cf", 0), (0, "a", 1), (1, "m1", 0), (0, "b", 0), (1, "a", 1),
+    (2, "m1", 0), (3, "cf", 0), (0, "b", 1), (3, "m1", 1), (0, "ad", 0), (1, "a", 0), (1, "b", 1), (3, "m1", 0),
+    (3, "a", 1), (0, "ad", 1), (2, "m1", 1), (1, "b", 0), (3, "a", 0), (1, "ad", 1), (3, "b", 1), (0, "e", 0),
+    (0, "e", 1), (1, "ad", 0), (3, "b", 0), (0, "f", 0), (2, "a", 1), (0, "f", 1), (1, "e", 1), (2, "a", 0),
+    (3, "ad", 1), (0, "m2", 0), (2, "b", 1), (1, "e", 0), (0, "m2", 1), (3, "ad", 0), (0, "gx", 0), (1, "f", 1),
+    (2, "b", 0), (1, "f", 0), (3, "e", 1), (0, "h", 0), (2, "ad", 1), (1, "m2", 1), (3, "e", 0), (1, "m2", 0),
+    (1, "gx", 0), (2, "ad", 0), (3, "f", 1), (3, "m2a", 1), (3, "f", 0), (1, "h", 0), (2, "e", 1), (3, "m2a", 0),
+    (3, "ga", 0), (0, "i", 0), (3, "m2b", 1), (2, "e", 0), (3, "ha", 0), (3, "m2b", 0), (3, "gb", 0), (2, "f", 1),
+    (2, "m2a", 1), (2, "f", 0), (3, "hb", 0), (2, "m2a", 0), (2, "ga", 0), (1, "i", 0), (2, "m2b", 1), (2, "ha", 0),
+    (2, "m2b", 0), (2, "gb", 0), (2, "hb", 0), (0, "o", 0), (3, "o", 0), (1, "o", 0), (2, "o", 0),
 ]
 
 

time: 90.8 us -> 89.7 us (0.988); the launches traced: 89.5 us -> 89.4 us
  no operation moved by 1% of the time
where the time goes in v4:
time: 89.7 us; the launch traced here: 89.4 us
  Pallas kernels  88.6 us (99%)
    pallas_call x1, Pallas kernels, on_device(): pl.pallas_call(kernel, out_shape=[pltpu.VMEM(*s) for s in shapes], in_spe...  87.6 us

profile of v4, /device:TPU:1, one launch (start us, length us, event | category | flops | bytes accessed | tf_op | source)
XLA Modules:
  0.0 89.4 jit_solution(14558655192337714081)
XLA Ops:
  0.6 87.6 %soap_step.1 = (f32[64,1600]{1,0:T(8,128)S(1)}, f32[64,1600]{1,0:T(8,128)S(1)}, bf16[64,1600]{1,0:T(8,128)(2,1)S(1)}) custom-call(bf16[64,1600]{1,0:T(8,128)(2,1)} %grad.1, bf16[1600,1600]{1,0:T(8,128)(2,1)} %basis.1, f32[64,1600]{1,0:T(8,128)} %moment.1, f32[64,1600]{1,0:T(8,128)} %second.1), custom_call_target="tpu_custom_call" | custom-call | flops 10485760000 | bytes 8388608 | tf_op jit(solution)/shard_map/soap_step/pallas_call | solution.py:401
  88.2 1.0 %flush.1 = (f32[64,1600]{1,0:T(8,128)}, f32[64,1600]{1,0:T(8,128)}, bf16[64,1600]{1,0:T(8,128)(2,1)}) custom-call(f32[64,1600]{1,0:T(8,128)S(1)} %get-tuple-element.6.a, f32[64,1600]{1,0:T(8,128)S(1)} %get-tuple-element.7.b, bf16[64,1600]{1,0:T(8,128)(2,1)S(1)} %get-tuple-element.8.c), custom_call_target="tpu_custom_call" | custom-call | tf_op jit(solution)/shard_map/flush/pallas_call | solution.py:420

commit v5 on v4

--- a/solution.py
+++ b/solution.py
@@ -25,9 +25,9 @@
     return [(j, min(256, start + size - j)) for j in range(start, start + size, 256)]
 
 
-ROWS = dict(g=112, cf=128, A=64, B=128, C=48, D=48, E1=64, E2=64, F=64, G=128, H=112, Y=96, I=16)
+ROWS = dict(g=112, cf=128, A=64, B=128, C=48, D=48, E1=64, E2=64, F=64, G=128, H=112, S=16, Y=96, I=16)
 KINDS = tuple(ROWS)
-WHOLE = ("g", "cf", "G", "H", "Y", "I")
+WHOLE = ("g", "cf", "G", "H", "S", "Y", "I")
 
 EARLY = (0, 1)
 
@@ -119,9 +119,18 @@
 
     def sent(kind):
         ref = part if kind == "G" else part16
-        chunks = {"H": Q - len(EARLY), "Y": len(EARLY), "I": len(EARLY)}.get(kind, Q)
-        span = ref.at[pl.ds(0, chunks), pl.ds(0, ROWS[kind])]
-        await_rows(send.at[KINDS.index(kind)], span)
+        chunks = {"H": Q - len(EARLY), "S": Q - len(EARLY), "Y": len(EARLY), "I": len(EARLY)}.get(kind, Q)
+
+        def wait(rows):
+            await_rows(send.at[KINDS.index(kind)], ref.at[pl.ds(0, chunks), pl.ds(0, rows)])
+
+        if kind == "H":
+            pl.when(y // 2 == core)(lambda: wait(96))
+            pl.when(y // 2 != core)(lambda: wait(128))
+        elif kind == "S":
+            pl.when(y // 2 == core)(lambda: wait(T))
+        else:
+            wait(ROWS[kind])
 
     def gather(q, j):
         own[q].wait()
@@ -267,32 +276,39 @@
             "G", recv_g.at[q, z], part.at[q, ds(slot(z * 2 + 1 - core), 64)], g_in.at[q, pl.ds(z * 64, 64)], sibling
         )
 
-    def add_core(q, z):
-        await_rows(recv_g.at[q, z], g_in.at[q, pl.ds(0, 64)])
-
-        def total(yy):
-            return part[q, ds(slot(z * 2 + core) + yy * T, T)] + g_in[q, ds(z * 64 + yy * T, T)]
-
+    def give_half(q, block):
+        put(
+            "G", recv_g.at[q, block], part.at[q, ds(block * 64 + (1 - core) * 32, 32)],
+            g_in.at[q, pl.ds(block * 32, 32)], sibling,
+        )
+
+    def add_half(q, block):
+        await_rows(recv_g.at[q, block], g_in.at[q, pl.ds(0, 32)])
+        dest = (x + block + 3) % 4
+        z, c = dest // 2, dest % 2
         other = (z + zlo) % 2
-        for d in range(4):
-            yy = (y + d) % 4
-
-            def pass_on(d=d, yy=yy):
-                at = z * 64 + d * T
-                h_out[q, ds(at, T)] = total(yy).astype(BF16)
+        for i in (0, 1):
+            yy = core * 2 + i
+            d = (yy + 4 - y) % 4
+            at = block * 32 + i * T
+            total = part[q, ds(block * 64 + core * 32 + i * T, T)] + g_in[q, at : at + T]
+            h_out[q, at : at + T] = total.astype(BF16)
+            here = jnp.logical_and(d == 0, other == 0)
+
+            @pl.when(jnp.logical_not(here))
+            def _(at=at, yy=yy, d=d):
                 put(
-                    "H", arrival("H", q), h_out.at[q, ds(at, T)], h_in.at[q, ds(other * 64 + d * T, T)],
-                    at_row(yy, z, core),
+                    "H", arrival("H", q), h_out.at[q, pl.ds(at, T)], h_in.at[q, ds(other * 64 + d * T, T)],
+                    at_row(yy, z, c),
                 )
 
-            if d:
-                pass_on()
-            else:
-                pl.when(other == 1)(pass_on)
-
-                @pl.when(other == 0)
-                def _():
-                    i_own[q] = total(y)
+            @pl.when(jnp.logical_and(here, c != core))
+            def _(at=at):
+                put("S", arrival("S", q), h_out.at[q, pl.ds(at, T)], h_in.at[q, pl.ds(0, T)], sibling)
+
+            @pl.when(jnp.logical_and(here, c == core))
+            def _(total=total):
+                i_own[q] = total
 
     def back_all(q, j):
         got("E2", q, j)
@@ -339,32 +355,36 @@
         back(q, j, 0, 192)
 
     def give_near(q, j):
-        for z in (0, 1):
-            pl.when(z * 2 + 1 - core != x_far)(lambda z=z: give_core(q, z))
+        for block in (0, 1, 2):
+            give_half(q, block)
 
     def add_near(q, j):
-        for z in (0, 1):
-            pl.when(z * 2 + core != x_far)(lambda z=z: add_core(q, z))
+        for block in (0, 1, 2):
+            add_half(q, block)
 
     def back_far(q, j):
         got("F", q, j)
         back(q, j, 192, 64)
 
     def give_far(q, j):
-        for z in (0, 1):
-            pl.when(z * 2 + 1 - core == x_far)(lambda z=z: give_core(q, z))
+        give_half(q, 3)
 
     def add_rest(q, j):
-        for z in (0, 1):
-            pl.when(z * 2 + core == x_far)(lambda z=z: add_core(q, z))
+        add_half(q, 3)
 
     def finish(q, j):
-        total = i_own[q]
         if q in EARLY:
             got("I", q)
-            total += i_in[q].astype(F32)
+            total = i_own[q] + i_in[q].astype(F32)
         else:
+
+            @pl.when(y // 2 != core)
+            def _():
+                got("S", q)
+                i_own[q] = h_in[q, pl.ds(0, T)].astype(F32)
+
             got("H", q)
+            total = i_own[q]
             for i in range(1, 8):
                 total += h_in[q, i * T : i * T + T].astype(F32)
         dv[q * T : q * T + T] = total.astype(BF16)
@@ -408,7 +428,7 @@
             vm(128, F32), vm(128), vm(32, F32), vm(128), vm(T, F32), vm(T), vm(T),
             pltpu.SemaphoreType.DMA((len(KINDS),)),
             pltpu.SemaphoreType.DMA((len(KINDS), Q, J)),
-            pltpu.SemaphoreType.DMA((Q, 2)),
+            pltpu.SemaphoreType.DMA((Q, 4)),
             pltpu.SemaphoreType.DMA((7,)),
         ],
         compiler_params=pltpu.CompilerParams(

time: 89.7 us -> 89.9 us (level)
  no operation moved by 1% of the time
where the time goes in v5:
time: 89.9 us; the launch traced here: 89.8 us
  Pallas kernels  89 us (99%)
    pallas_call x1, Pallas kernels, on_device(): pl.pallas_call(kernel, out_shape=[pltpu.VMEM(*s) for s in shapes], in_spe...  88.1 us

profile of v5, /device:TPU:1, one launch (start us, length us, event | category | flops | bytes accessed | tf_op | source)
XLA Modules:
  0.0 89.8 jit_solution(6192816849314788870)
XLA Ops:
  0.6 88.1 %soap_step.1 = (f32[64,1600]{1,0:T(8,128)S(1)}, f32[64,1600]{1,0:T(8,128)S(1)}, bf16[64,1600]{1,0:T(8,128)(2,1)S(1)}) custom-call(bf16[64,1600]{1,0:T(8,128)(2,1)} %grad.1, bf16[1600,1600]{1,0:T(8,128)(2,1)} %basis.1, f32[64,1600]{1,0:T(8,128)} %moment.1, f32[64,1600]{1,0:T(8,128)} %second.1), custom_call_target="tpu_custom_call" | custom-call | flops 10485760000 | bytes 8388608 | tf_op jit(solution)/shard_map/soap_step/pallas_call | solution.py:421
  88.7 1.0 %flush.1 = (f32[64,1600]{1,0:T(8,128)}, f32[64,1600]{1,0:T(8,128)}, bf16[64,1600]{1,0:T(8,128)(2,1)}) custom-call(f32[64,1600]{1,0:T(8,128)S(1)} %get-tuple-element.6.a, f32[64,1600]{1,0:T(8,128)S(1)} %get-tuple-element.7.b, bf16[64,1600]{1,0:T(8,128)(2,1)S(1)} %get-tuple-element.8.c), custom_call_target="tpu_custom_call" | custom-call | tf_op jit(solution)/shard_map/flush/pallas_call | solution.py:440
